TPU v7x, 32 devices: a whole 2x2x4 slice. The times are simulated.
32 devices in a mesh: row: 8 (over y, x, core), col: 4 (over z).
Axes of the slice: x: 2, y: 2, z: 4, core: 2. Of those that a mesh axis runs over, the one named last changes fastest.
Arguments:
- positions: bfloat16 [3, 49152], P(None, 'row'), may hold values from -3.3 to 3.3, as said below
- normals: bfloat16 [3, 49152], P(None, 'row'), may hold values from -1 to 1, as said below
- areas: bfloat16 [49152], P('row'), as said below
- radiosity: bfloat16 [32, 49152], P(None, 'row'), may hold values from 0.19921875 to 5
- reflect: float32 [49152], P('row'), may hold values from 0.2 to 0.9
- partial_sums: float32 [128, 49152], P('col', 'row'), may hold values from -6 to 6
- visible: int32 [384, 384], P('row'), may hold values 0 or 1
- section: int32 [1], replicated, may hold values from 0 to 7
Outputs:
- advanced: float32 [128, 49152], P('col', 'row')
Inputs may be any that keep to these rules, and one draw needn't show every extreme that they name: `positions`: patches of one block lie around a common centre. `normals`: each column has length close to 1. `areas`: each area is positive; 6144 times an area lies between 51 and 1640.
All inputs are finite; a program needn't handle non-finite values. No bound on the sum of `visible` on one device may be relied on, other than what follows from the above.
Results may differ from a plain program's by a relative error of at most 0.0003.
Values may be sent and summed in bfloat16 or wider, within the bound.
No kernel may reach another device: no remote copies, remote signals or barrier semaphores. Data moves between devices by JAX's collectives and lax.ppermute only.
A program may use at most 64 MiB of HBM per device.

v0:
```python
import functools
import math

import jax
import jax.numpy as jnp
from jax import lax
from jax.experimental import pallas as pl
from jax.experimental.pallas import tpu as pltpu
from jax.sharding import PartitionSpec as P

BF = jnp.bfloat16
F32 = jnp.float32
TILE = 128
CHUNK = 16
FEATURES = 48
BITS = 6
STEP = 16
BUILD = 4
RECEIVE = 8
FROM_PRODUCT = (True, True, False)
KAPPA = (math.pi - 1) / (2 * math.pi)
SIGMA = (math.pi + 1) / (2 * math.pi)


def visible_pairs(mask):
    n_rec, n_em = mask.shape
    cum = jnp.cumsum(mask, axis=1)
    pairs = (cum[:, -1] + 1) // 2
    ends = jnp.cumsum(pairs)
    q = jnp.arange(n_rec * ((n_em + 1) // 2) + 2 * STEP, dtype=jnp.int32)
    a = jnp.sum((ends[None, :] <= q[:, None]).astype(jnp.int32), axis=1)
    hot = a[:, None] == jnp.arange(n_rec, dtype=jnp.int32)[None, :]
    rows = jnp.dot(hot.astype(F32), cum.astype(F32), preferred_element_type=F32)
    first = jnp.sum(jnp.where(hot, (ends - pairs)[None, :], 0), axis=1)
    rank = (2 * (q - first)).astype(F32)
    code = jnp.minimum(a, n_rec - 1)
    for t in range(2):
        code = (code << BITS) + jnp.sum((rows <= rank[:, None] + t).astype(jnp.int32), axis=1)
    return ends[-1:], code


def decoded(code):
    last = (1 << BITS) - 1
    return code >> (2 * BITS), [(code >> BITS) & last, code & last]


def lanes(tile):
    return pl.ds(pl.multiple_of(tile * TILE, TILE), TILE)


def rounded(x):
    return x.astype(BF).astype(F32)


def term_kernel(count, codes, own, *refs):
    pieces, (out, feat, rows, rad, rec, place, view) = refs[:-7], refs[-7:]
    cases = out.shape[0]
    n_rec, n_em = own.shape[1] // TILE, rad.shape[1] // TILE - 1
    steps = (count[0] + STEP - 1) // STEP
    out[...] = jnp.zeros_like(out)
    view[...] = jnp.zeros_like(view)
    feat[:, n_em * TILE :] = jnp.zeros((FEATURES, TILE), BF)
    rows[:, n_em * TILE :] = jnp.zeros((8, TILE), F32)
    rad[:, n_em * TILE :] = jnp.zeros((cases, TILE), BF)

    def build(piece, start, k):
        width = BUILD * TILE if piece.shape[1] % (BUILD * TILE) == 0 else TILE
        taken = pl.ds(pl.multiple_of(k * width, width), width)
        at = pl.ds(pl.multiple_of(start + k * width, TILE), width)
        rad[:, at] = piece[:cases, taken]
        geo = piece[cases:, taken].astype(F32)
        row = lax.broadcasted_iota(jnp.int32, geo.shape, 0)
        px, py, pz, nx, ny, nz, area = (geo[i : i + 1] for i in range(7))
        scale = 1.0 / (KAPPA * area)
        main = geo * (scale * jnp.where(row < 3, -2.0, 1.0 / (math.pi * KAPPA)))
        middle = scale * (px * px + py * py + pz * pz) + SIGMA / KAPPA
        own = (nx * px + ny * py + nz * pz) * scale * (-1.0 / (math.pi * KAPPA))
        main = jnp.where(row < 6, main, jnp.where(row == 6, middle, own))
        high = rounded(main)
        mid = rounded(main - high)
        s_high = rounded(scale)
        s_mid = rounded(scale - s_high)
        s_low = scale - s_high - s_mid
        scales = jnp.where(row < 3, s_high, jnp.where(row < 5, s_mid, s_low))
        scales = jnp.where(row < 6, scales, 1.0)
        geo = jnp.where(row == 7, 1.0, geo)
        parts = [high, mid, main - high - mid, scales, geo, jnp.zeros_like(geo)]
        feat[:, at] = jnp.concatenate(parts, 0).astype(BF)
        rows[:, at] = main

    start = 0
    for piece in pieces:
        columns = piece.shape[1]
        count_here = columns // (BUILD * TILE if columns % (BUILD * TILE) == 0 else TILE)

        def build_here(k, carry, piece=piece, start=start):
            build(piece, start, k)
            return carry

        lax.fori_loop(0, count_here, build_here, 0, unroll=True)
        start += columns

    turn = jnp.where(
        lax.broadcasted_iota(jnp.int32, (TILE, TILE), 0)
        == lax.broadcasted_iota(jnp.int32, (TILE, TILE), 1),
        1.0,
        0.0,
    ).astype(BF)

    def receive(a, carry):
        geo = own[:, lanes(a)].astype(F32)
        row = lax.broadcasted_iota(jnp.int32, geo.shape, 0)
        none = jnp.zeros_like(geo)
        px, py, pz, nx, ny, nz = (geo[i : i + 1] for i in range(6))
        square = px * px + py * py + pz * pz
        s_high = rounded(square)
        s_mid = rounded(square - s_high)
        s_low = square - s_high - s_mid
        back = -(nx * px + ny * py + nz * pz)
        b_high = rounded(back)
        b_mid = rounded(back - b_high)
        b_low = back - b_high - b_mid
        first = jnp.where(row < 3, geo, jnp.where(row == 6, 1.0, 0.0))
        second = jnp.where(row % 3 == 0, s_high, jnp.where(row % 3 == 1, s_mid, s_low))
        second = jnp.where(row < 5, second, jnp.where(row == 5, s_high, 0.0))
        wide = jnp.concatenate([first, first, first, second, none, none], 0)
        high = jnp.where(row == 6, b_high, jnp.where(row == 7, b_mid, 0.0))
        low = jnp.concatenate([nx, ny, nz] + [none[:4]] + [b_low], 0)
        facing = jnp.concatenate([none, none, none, high, low, none], 0)
        shift = jnp.concatenate([none[:3], px, py, pz, none[:1], none[:1] + 1.0], 0)
        lit = jnp.concatenate([shift, shift, shift, none, none, none], 0)
        for kind, f in enumerate((wide, facing, lit)):
            columns = lax.dot_general(
                turn, f.astype(BF), (((1,), (1,)), ((), ())), preferred_element_type=F32
            )
            if kind == 0:
                place[a] = columns
            columns = columns.astype(BF)
            for k in range(TILE // CHUNK):
                at = (3 * k + kind) * CHUNK
                rec[a, at : at + CHUNK] = columns[k * CHUNK : (k + 1) * CHUNK]
        return carry

    lax.fori_loop(0, n_rec, receive, 0, unroll=RECEIVE if n_rec % RECEIVE == 0 else 1)

    def views(a, tiles, slot):
        product_cos = FROM_PRODUCT[slot % len(FROM_PRODUCT)]
        kinds = 3 if product_cos else 2
        left = jnp.concatenate(
            [
                rec[a, 3 * r : 3 * r + kinds * CHUNK]
                for r in range(0, TILE, CHUNK)
            ],
            axis=0,
        )
        right = jnp.concatenate([feat[:, lanes(b)] for b in tiles], axis=1)
        products = jnp.dot(left, right, preferred_element_type=F32)
        emit = [rows[:, lanes(b)] for b in tiles]
        for r in range(0, TILE, CHUNK):
            if not product_cos:
                x, y, z = (
                    jnp.broadcast_to(place[a, r : r + CHUNK, k : k + 1], (CHUNK, TILE))
                    for k in range(3)
                )
            for t in range(2):
                m = products[kinds * r : kinds * (r + CHUNK), t * TILE : (t + 1) * TILE]
                if product_cos:
                    cos = m[2 * CHUNK :]
                else:
                    e = emit[t]
                    cos = e[3:4] * x + e[4:5] * y + e[5:6] * z + e[7:8]
                w = m[:CHUNK]
                v = jnp.maximum(cos, 0.0) * m[CHUNK : 2 * CHUNK]
                v = v * pltpu.reciprocal(w * w - 1.0, approx=True)
                at = slice(t * TILE, (t + 1) * TILE)
                view[slot, r : r + CHUNK, at] = jnp.maximum(v.astype(BF), 0)

    def add(a, tiles, slot):
        radiated = jnp.concatenate([rad[:, lanes(b)] for b in tiles], axis=1)
        out[:, lanes(a)] += lax.dot_general(
            radiated, view[slot], (((1,), (1,)), ((), ())), preferred_element_type=F32
        )

    def step(i, carry):
        for j in range(STEP):
            add(*decoded(codes[jnp.maximum(i - 1, 0) * STEP + j]), j)
            views(*decoded(codes[i * STEP + j]), j)
        return carry

    lax.fori_loop(0, steps, step, 0)
    for j in range(STEP):
        add(*decoded(codes[jnp.maximum(steps - 1, 0) * STEP + j]), j)


def block_term(count, codes, own, *pieces):
    cases = pieces[0].shape[0] - own.shape[0]
    columns = sum(piece.shape[1] for piece in pieces)
    tiles = own.shape[1] // TILE
    smem = pl.BlockSpec(memory_space=pltpu.SMEM)
    vmem = pl.BlockSpec(memory_space=pltpu.VMEM)
    pairs = tiles * TILE * columns
    return pl.pallas_call(
        term_kernel,
        out_shape=jax.ShapeDtypeStruct((cases, tiles * TILE), F32),
        in_specs=[smem] * 2 + [vmem] * (1 + len(pieces)),
        out_specs=vmem,
        scratch_shapes=[
            pltpu.VMEM((FEATURES, columns + TILE), BF),
            pltpu.VMEM((8, columns + TILE), F32),
            pltpu.VMEM((cases, columns + TILE), BF),
            pltpu.VMEM((tiles, 3 * TILE, FEATURES), BF),
            pltpu.VMEM((tiles, TILE, FEATURES), F32),
            pltpu.VMEM((STEP, TILE, 2 * TILE), BF),
        ],
        compiler_params=pltpu.CompilerParams(vmem_limit_bytes=24 * 2**20),
        cost_estimate=pl.CostEstimate(
            flops=pairs * 300, bytes_accessed=8 * 2**20, transcendentals=pairs
        ),
        name="block_term",
    )(count, codes, own, *pieces)


def exchanged(block, axis, bits):
    return lax.ppermute(block, axis, [(i, i ^ bits) for i in range(lax.axis_size(axis))])


def spread_from(root, axis, wide, narrow):
    n = lax.axis_size(axis)
    me = lax.axis_index(axis)
    away, odd = me ^ root, me & 1
    wide = jnp.where(away & 1 == 0, wide, exchanged(wide, axis, 1))
    narrow = jnp.where(away & 1 == 0, narrow, exchanged(narrow, axis, 1))
    block = jnp.concatenate([wide, narrow], 0)
    q = block.shape[1] // 4
    parts = [
        jnp.where(odd == 0, block[:, i * q : (i + 1) * q], block[:, (i + 2) * q : (i + 3) * q])
        for i in range(2)
    ]
    bits = [1 << i for i in range(1, n.bit_length() - 1)]
    for pair in zip(bits, bits[::-1]):
        got = [exchanged(part, axis, bit) for part, bit in zip(parts, pair)]
        parts = [jnp.where(away & bit == 0, x, y) for x, y, bit in zip(parts, got, pair)]
    mine = jnp.concatenate(parts, axis=1)
    return mine, exchanged(mine, axis, 1)


def shifted(block, axis, distance):
    n = lax.axis_size(axis)
    return lax.ppermute(block, axis, [((i - distance) % n, i) for i in range(n)])


def on_device(positions, normals, areas, radiosity, reflect, partial_sums, visible, section):
    n_row = lax.axis_size("row")
    emit = (lax.axis_index("col") + section[0]) % n_row
    tiles = positions.shape[1] // TILE
    own = jnp.concatenate([positions, normals, areas[None], areas[None]], 0)
    pieces = spread_from(emit, "row", radiosity, own)
    carried = shifted(partial_sums, "col", 1)
    mask = lax.dynamic_slice_in_dim(visible, emit * tiles, tiles, 1)
    half = tiles // 2
    swapped = jnp.concatenate([mask[:, half:], mask[:, :half]], 1)
    mask = jnp.where(lax.axis_index("row") & 1 == 0, mask, swapped)
    count, codes = visible_pairs(mask)
    return carried + reflect[None, :] * block_term(count, codes, own, *pieces)


def solution(mesh):
    placed = (
        P(None, "row"),
        P(None, "row"),
        P("row"),
        P(None, "row"),
        P("row"),
        P("col", "row"),
        P("row", None),
        P(),
    )
    return jax.shard_map(
        on_device, mesh=mesh, in_specs=placed, out_specs=P("col", "row"), check_vma=False
    )
```

profile of v0, /device:TPU:0, one launch (start us, length us, event | category | flops | bytes accessed | tf_op | source)
XLA Modules:
  0.0 81.8 jit_solution(10856286458155764118)
XLA Ops:
  0.0 0.7 broadcast_in_dim.16
  0.7 0.0 copy-start.1
  0.7 1.0 %pad_maximum_fusion.2.own = bf16[8,6144]{1,0:T(8,128)(2,1)S(1)} fusion(bf16[1,6144]{1,0:T(2,128)(2,1)S(1)} %broadcast_in_dim.16, bf16[3,6144]{1,0:T(4,128)(2,1)} %param.9, bf16[3,6144]{1,0:T(4,128)(2,1)} %param.8), kind=kLoop, calls=%fused_computation.27 | loop fusion | flops 393216 | bytes 184320 | tf_op jit(solution)/shard_map/concatenate | solution.py:256
  1.7 0.5 collective-permute-start.2
  2.2 0.1 collective-permute-start.1
  2.3 3.0 %collective-permute-start = (f32[32,6144]{1,0:T(8,128)}, f32[32,6144]{1,0:T(8,128)S(1)}, u32[]{:S(2)}, u32[]{:S(2)}) collective-permute-start(f32[32,6144]{1,0:T(8,128)} %param.13), channel_id=1, source_target_pairs={{3,0},{0,1},{1,2},{2,3},{7,4},{4,5},{5,6},{6,7},{11,8},{8,9},{9,10... | collective-permute-start | bytes 2359304 | tf_op jit(solution)/shard_map/ppermute | solution.py:249
  6.1 0.1 constant_dynamic-slice_fusion
  6.1 0.1 add_select_fusion.1
  6.2 0.2 reduce_window_sum.18
  6.4 0.2 fusion.10
  6.6 0.1 reduce-window.4
  6.7 0.1 reduce
  6.8 0.1 convert_reduce_fusion.2
  7.0 0.1 select_reduce_fusion
  7.1 0.0 collective-permute-done.2
  7.1 0.0 collective-permute-done.1
  7.2 0.1 fusion.4
  7.3 1.6 %collective-permute-start.3 = (bf16[40,1536]{1,0:T(8,128)(2,1)S(1)}, bf16[40,1536]{1,0:T(8,128)(2,1)S(1)}, u32[]{:S(2)}, u32[]{:S(2)}) collective-permute-start(bf16[40,1536]{1,0:T(8,128)(2,1)S(1)} %get-tuple-element.7), channel_id=1, source_target_pairs={{0,8},{4,12},{8,0},{12,4},{16,24},{20,28},{24,16},{28,20},{1,9},{5... | collective-permute-start | bytes 368648 | tf_op jit(solution)/shard_map/ppermute | solution.py:224
  8.8 1.5 %collective-permute-start.5 = (bf16[40,1536]{1,0:T(8,128)(2,1)S(1)}, bf16[40,1536]{1,0:T(8,128)(2,1)S(1)}, u32[]{:S(2)}, u32[]{:S(2)}) collective-permute-start(bf16[40,1536]{1,0:T(8,128)(2,1)S(1)} %get-tuple-element.8), channel_id=1, source_target_pairs={{0,16},{4,20},{8,24},{12,28},{16,0},{20,4},{24,8},{28,12},{1,17},{... | collective-permute-start | bytes 368648 | tf_op jit(solution)/shard_map/ppermute | solution.py:224
  10.4 2.0 %collective-permute-done.3 = bf16[40,1536]{1,0:T(8,128)(2,1)S(1)} collective-permute-done((bf16[40,1536]{1,0:T(8,128)(2,1)S(1)}, bf16[40,1536]{1,0:T(8,128)(2,1)S(1)}, u32[]{:S(2)}, u32[]{:S(2)}) %collective-permute-start.3) | collective-permute-done | bytes 122912 | tf_op jit(solution)/shard_map/ppermute | solution.py:224
  12.4 1.6 %collective-permute-start.4 = (bf16[40,1536]{1,0:T(8,128)(2,1)S(1)}, bf16[40,1536]{1,0:T(8,128)(2,1)S(1)}, u32[]{:S(2)}, u32[]{:S(2)}) collective-permute-start(bf16[40,1536]{1,0:T(8,128)(2,1)S(1)} %broadcast_select_fusion.2), channel_id=1, source_target_pairs={{0,16},{4,20},{8,24},{12,28},{16,0},{20,4},{24,8},{28,12},{1,17},{... | collective-permute-start | bytes 368648 | tf_op jit(solution)/shard_map/ppermute | solution.py:224
  14.0 0.0 collective-permute-done.5
  14.0 1.6 %collective-permute-start.6 = (bf16[40,1536]{1,0:T(8,128)(2,1)S(1)}, bf16[40,1536]{1,0:T(8,128)(2,1)S(1)}, u32[]{:S(2)}, u32[]{:S(2)}) collective-permute-start(bf16[40,1536]{1,0:T(8,128)(2,1)S(1)} %broadcast_select_fusion.3), channel_id=1, source_target_pairs={{0,8},{4,12},{8,0},{12,4},{16,24},{20,28},{24,16},{28,20},{1,9},{5... | collective-permute-start | bytes 368648 | tf_op jit(solution)/shard_map/ppermute | solution.py:224
  15.5 1.8 %collective-permute-done.4 = bf16[40,1536]{1,0:T(8,128)(2,1)S(1)} collective-permute-done((bf16[40,1536]{1,0:T(8,128)(2,1)S(1)}, bf16[40,1536]{1,0:T(8,128)(2,1)S(1)}, u32[]{:S(2)}, u32[]{:S(2)}) %collective-permute-start.4) | collective-permute-done | bytes 122912 | tf_op jit(solution)/shard_map/ppermute | solution.py:224
  17.3 1.6 %collective-permute-done.6 = bf16[40,1536]{1,0:T(8,128)(2,1)S(1)} collective-permute-done((bf16[40,1536]{1,0:T(8,128)(2,1)S(1)}, bf16[40,1536]{1,0:T(8,128)(2,1)S(1)}, u32[]{:S(2)}, u32[]{:S(2)}) %collective-permute-start.6) | collective-permute-done | bytes 122912 | tf_op jit(solution)/shard_map/ppermute | solution.py:224
  19.0 0.1 collective-permute-start.7
  19.1 0.3 convert_reduce_fusion.1
  19.3 0.5 slice.37
  19.9 0.7 collective-permute-done.7.refs_1_
  20.6 60.1 %block_term.1 = f32[32,6144]{1,0:T(8,128)S(1)} custom-call(s32[1]{0:T(128)} %bitcast.1.count, s32[1184]{0:T(1024)S(1)} %shift-left_add_fusion.codes, bf16[8,6144]{1,0:T(8,128)(2,1)S(1)} %pad_maximum_fusion.2.own, bf16[40,3072]{1,0:T(8,128)(2,1)S(1)} %pad_maximum_fusion.refs_0_, bf16[40,3072]{1,0:T(8,128)(2,1)S(1)} %collective-permute-done.7.refs_1_), custom_call_target="tpu_custom_call" | custom-call | flops 11324620800 | bytes 8388608 | tf_op jit(solution)/shard_map/block_term/pallas_call | solution.py:202
  80.7 0.0 collective-permute-done
  80.7 1.0 %multiply_add_fusion = f32[32,6144]{1,0:T(8,128)} fusion(f32[32,6144]{1,0:T(8,128)S(1)} %collective-permute-done, f32[32,6144]{1,0:T(8,128)S(1)} %block_term.1, f32[6144]{0:T(1024)S(1)} %copy-done.2), kind=kLoop, calls=%fused_computation | loop fusion | flops 393216 | bytes 2383872 | tf_op jit(solution)/shard_map/add | solution.py:264
  (16 shorter events, 0.2 us)
Async XLA Ops:
  0.7 5.3 %copy-start.1 = (s32[48,384]{1,0:T(8,128)S(1)}, s32[48,384]{1,0:T(8,128)}, u32[]{:S(2)}) copy-start(s32[48,384]{1,0:T(8,128)} %param.14) | copy-start | bytes 221188
  1.7 5.4 %collective-permute-start.2 = (bf16[8,6144]{1,0:T(8,128)(2,1)S(1)}, bf16[8,6144]{1,0:T(8,128)(2,1)S(1)}, u32[]{:S(2)}, u32[]{:S(2)}) collective-permute-start(bf16[8,6144]{1,0:T(8,128)(2,1)S(1)} %pad_maximum_fusion.2.own), channel_id=1, source_target_pairs={{0,4},{4,0},{8,12},{12,8},{16,20},{20,16},{24,28},{28,24},{1,5},{5... | collective-permute-start | bytes 294920 | tf_op jit(solution)/shard_map/ppermute | solution.py:224
  2.2 4.9 %collective-permute-start.1 = (bf16[32,6144]{1,0:T(8,128)(2,1)}, bf16[32,6144]{1,0:T(8,128)(2,1)S(1)}, u32[]{:S(2)}, u32[]{:S(2)}) collective-permute-start(bf16[32,6144]{1,0:T(8,128)(2,1)} %param.11), channel_id=1, source_target_pairs={{0,4},{4,0},{8,12},{12,8},{16,20},{20,16},{24,28},{28,24},{1,5},{5... | collective-permute-start | bytes 1179656 | tf_op jit(solution)/shard_map/ppermute | solution.py:224
  2.3 78.4 %collective-permute-start = (f32[32,6144]{1,0:T(8,128)}, f32[32,6144]{1,0:T(8,128)S(1)}, u32[]{:S(2)}, u32[]{:S(2)}) collective-permute-start(f32[32,6144]{1,0:T(8,128)} %param.13), channel_id=1, source_target_pairs={{3,0},{0,1},{1,2},{2,3},{7,4},{4,5},{5,6},{6,7},{11,8},{8,9},{9,10... | collective-permute-start | bytes 2359304 | tf_op jit(solution)/shard_map/ppermute | solution.py:249
  5.3 1.8 %copy-start = (bf16[32,6144]{1,0:T(8,128)(2,1)S(1)}, bf16[32,6144]{1,0:T(8,128)(2,1)}, u32[]{:S(2)}) copy-start(bf16[32,6144]{1,0:T(8,128)(2,1)} %param.11) | copy-start | bytes 1179652
  7.3 5.1 %collective-permute-start.3 = (bf16[40,1536]{1,0:T(8,128)(2,1)S(1)}, bf16[40,1536]{1,0:T(8,128)(2,1)S(1)}, u32[]{:S(2)}, u32[]{:S(2)}) collective-permute-start(bf16[40,1536]{1,0:T(8,128)(2,1)S(1)} %get-tuple-element.7), channel_id=1, source_target_pairs={{0,8},{4,12},{8,0},{12,4},{16,24},{20,28},{24,16},{28,20},{1,9},{5... | collective-permute-start | bytes 368648 | tf_op jit(solution)/shard_map/ppermute | solution.py:224
  8.8 5.1 %collective-permute-start.5 = (bf16[40,1536]{1,0:T(8,128)(2,1)S(1)}, bf16[40,1536]{1,0:T(8,128)(2,1)S(1)}, u32[]{:S(2)}, u32[]{:S(2)}) collective-permute-start(bf16[40,1536]{1,0:T(8,128)(2,1)S(1)} %get-tuple-element.8), channel_id=1, source_target_pairs={{0,16},{4,20},{8,24},{12,28},{16,0},{20,4},{24,8},{28,12},{1,17},{... | collective-permute-start | bytes 368648 | tf_op jit(solution)/shard_map/ppermute | solution.py:224
  12.4 4.9 %collective-permute-start.4 = (bf16[40,1536]{1,0:T(8,128)(2,1)S(1)}, bf16[40,1536]{1,0:T(8,128)(2,1)S(1)}, u32[]{:S(2)}, u32[]{:S(2)}) collective-permute-start(bf16[40,1536]{1,0:T(8,128)(2,1)S(1)} %broadcast_select_fusion.2), channel_id=1, source_target_pairs={{0,16},{4,20},{8,24},{12,28},{16,0},{20,4},{24,8},{28,12},{1,17},{... | collective-permute-start | bytes 368648 | tf_op jit(solution)/shard_map/ppermute | solution.py:224
  14.0 4.9 %collective-permute-start.6 = (bf16[40,1536]{1,0:T(8,128)(2,1)S(1)}, bf16[40,1536]{1,0:T(8,128)(2,1)S(1)}, u32[]{:S(2)}, u32[]{:S(2)}) collective-permute-start(bf16[40,1536]{1,0:T(8,128)(2,1)S(1)} %broadcast_select_fusion.3), channel_id=1, source_target_pairs={{0,8},{4,12},{8,0},{12,4},{16,24},{20,28},{24,16},{28,20},{1,9},{5... | collective-permute-start | bytes 368648 | tf_op jit(solution)/shard_map/ppermute | solution.py:224
  19.0 1.6 %collective-permute-start.7 = (bf16[40,3072]{1,0:T(8,128)(2,1)S(1)}, bf16[40,3072]{1,0:T(8,128)(2,1)S(1)}, u32[]{:S(2)}, u32[]{:S(2)}) collective-permute-start(bf16[40,3072]{1,0:T(8,128)(2,1)S(1)} %pad_maximum_fusion.refs_0_), channel_id=1, source_target_pairs={{0,4},{4,0},{8,12},{12,8},{16,20},{20,16},{24,28},{28,24},{1,5},{5... | collective-permute-start | bytes 737288 | tf_op jit(solution)/shard_map/ppermute | solution.py:224
  20.6 60.2 %copy-start.2 = (f32[6144]{0:T(1024)S(1)}, f32[6144]{0:T(1024)}, u32[]{:S(2)}) copy-start(f32[6144]{0:T(1024)} %param.12) | copy-start | bytes 73732
where the time goes:
time: 82.5 us; the launch traced here: 81.8 us
  Pallas kernels  60.1 us (73%)
  starting transfers between devices  9.89 us (12%)
  waiting for transfers between devices  6.09 us (7%)
  other arithmetic  3.12 us (4%)
  local copies, waits for them, and re-layouts  1.33 us (2%)
  between operations  0.91 us (1%)
    pallas_call x1, Pallas kernels, block_term(): pl.pallas_call(term_kernel, out_shape=jax.ShapeDtypeStruct((cases, tiles...  60.1 us
    ppermute x7, starting transfers between devices, exchanged(): lax.ppermute(block, axis, [(i, i ^ bits) for i in range(lax.axis_size(axi...  6.88 us
    ppermute x7, waiting for transfers between devices, exchanged(): lax.ppermute(block, axis, [(i, i ^ bits) for i in range(lax.axis_size(axi...  6.09 us
    ppermute x1, starting transfers between devices, shifted(): lax.ppermute(block, axis, [((i - distance) % n, i) for i in range(n)])  3 us
  transfers between devices with their start and end apart: 8, of which 4 were waited for; matrix products, arithmetic and copies ran while one was open for 2% of the time, Pallas kernels for 74%

commit v1 on v0

v1 whole, which is shorter than its diff:
```python
import functools
import math

import jax
import jax.numpy as jnp
from jax import lax
from jax.experimental import pallas as pl
from jax.experimental.pallas import tpu as pltpu
from jax.sharding import PartitionSpec as P

BF = jnp.bfloat16
F32 = jnp.float32
TILE = 128
CHUNK = 16
FEATURES = 48
BITS = 6
STEP = 24
BUILD = 4
UNROLL = 24
FROM_PRODUCT = (True, True, False)
KAPPA = (math.pi - 1) / (2 * math.pi)
SIGMA = (math.pi + 1) / (2 * math.pi)


def visible_pairs(mask):
    n_rec, n_em = mask.shape
    cum = jnp.cumsum(mask.T, axis=1)
    pairs = (cum[:, -1] + 1) // 2
    ends = jnp.cumsum(pairs)
    q = jnp.arange(n_em * ((n_rec + 1) // 2) + 2 * STEP, dtype=jnp.int32)
    b = jnp.sum((ends[None, :] <= q[:, None]).astype(jnp.int32), axis=1)
    hot = b[:, None] == jnp.arange(n_em, dtype=jnp.int32)[None, :]
    rows = jnp.dot(hot.astype(F32), cum.astype(F32), preferred_element_type=F32)
    first = jnp.sum(jnp.where(hot, (ends - pairs)[None, :], 0), axis=1)
    rank = (2 * (q - first)).astype(F32)
    code = jnp.minimum(b, n_em - 1)
    for t in range(2):
        code = (code << BITS) + jnp.sum((rows <= rank[:, None] + t).astype(jnp.int32), axis=1)
    return ends[-1:], code


def decoded(code):
    last = (1 << BITS) - 1
    return code >> (2 * BITS), [(code >> BITS) & last, code & last]


def lanes(tile):
    return pl.ds(pl.multiple_of(tile * TILE, TILE), TILE)


def rounded(x):
    return x.astype(BF).astype(F32)


def term_kernel(count, codes, own, *refs):
    pieces, (out, feat, rows, rad, em, place, view) = refs[:-7], refs[-7:]
    cases = out.shape[0]
    n_rec, n_em = own.shape[1] // TILE, rad.shape[1] // TILE
    steps = (count[0] + STEP - 1) // STEP
    out[...] = jnp.zeros_like(out)
    view[...] = jnp.zeros_like(view)
    feat[:, n_rec * TILE :] = jnp.zeros((FEATURES, TILE), BF)
    rows[:, n_rec * TILE :] = jnp.zeros((8, TILE), F32)

    width = BUILD * TILE if n_rec % BUILD == 0 else TILE

    def receivers(k, carry):
        at = pl.ds(pl.multiple_of(k * width, width), width)
        geo = own[:, at].astype(F32)
        row = lax.broadcasted_iota(jnp.int32, geo.shape, 0)
        px, py, pz, nx, ny, nz = (geo[i : i + 1] for i in range(6))
        square = px * px + py * py + pz * pz
        back = -(nx * px + ny * py + nz * pz)
        full = jnp.where(row < 3, square, back)
        high = rounded(full)
        mid = rounded(full - high)
        low = full - high - mid
        parts = jnp.where(row % 3 == 0, high, jnp.where(row % 3 == 1, mid, low))
        parts = jnp.where(row < 6, parts, 0.0)
        plain = jnp.where(row < 6, geo, jnp.where(row == 6, 1.0, 0.0))
        feat[:, at] = jnp.concatenate([plain] * 3 + [parts] * 3, 0).astype(BF)
        rows[:, at] = jnp.where(row == 6, back, plain)
        return carry

    lax.fori_loop(0, n_rec * TILE // width, receivers, 0, unroll=True)

    turn = jnp.where(
        lax.broadcasted_iota(jnp.int32, (TILE, TILE), 0)
        == lax.broadcasted_iota(jnp.int32, (TILE, TILE), 1),
        1.0,
        0.0,
    ).astype(BF)

    def emitters(piece, start, b):
        rad[:, lanes(start + b)] = piece[:cases, lanes(b)]
        geo = piece[cases:, lanes(b)].astype(F32)
        row = lax.broadcasted_iota(jnp.int32, geo.shape, 0)
        none = jnp.zeros_like(geo)
        px, py, pz, nx, ny, nz, area = (geo[i : i + 1] for i in range(7))
        scale = 1.0 / (KAPPA * area)
        main = geo * (scale * jnp.where(row < 3, -2.0, 1.0 / (math.pi * KAPPA)))
        middle = scale * (px * px + py * py + pz * pz) + SIGMA / KAPPA
        behind = (nx * px + ny * py + nz * pz) * scale * (-1.0 / (math.pi * KAPPA))
        main = jnp.where(row < 6, main, jnp.where(row == 6, middle, behind))
        high = rounded(main)
        mid = rounded(main - high)
        thirds = [high, mid, main - high - mid]
        s_high = rounded(scale)
        s_mid = rounded(scale - s_high)
        s_low = scale - s_high - s_mid
        w_row = (row < 3) | (row == 6)
        wide = [jnp.where(w_row, x, 0.0) for x in thirds]
        wide += [jnp.where(row < 3 - i, x, 0.0) for i, x in enumerate((s_high, s_mid, s_low))]
        lit = [
            jnp.concatenate([x[3:6], none[:3], x[7:8], none[:1]], 0) for x in thirds
        ] + [none] * 3
        spot = jnp.concatenate([none[:3], px, py, pz, none[:2]], 0)
        ones = jnp.where((row >= 3) & (row < 6), 1.0, 0.0)
        facing = [spot, none, none, ones, none, none]
        for kind, f in enumerate((wide, lit, facing)):
            f = jnp.concatenate(f, 0).astype(BF)
            columns = lax.dot_general(
                turn, f, (((1,), (1,)), ((), ())), preferred_element_type=F32
            )
            if kind == 2:
                place[start + b] = columns
            columns = columns.astype(BF)
            for k in range(TILE // CHUNK):
                at = (3 * k + kind) * CHUNK
                em[start + b, at : at + CHUNK] = columns[k * CHUNK : (k + 1) * CHUNK]

    start = 0
    for piece in pieces:
        tiles_here = piece.shape[1] // TILE

        def emitters_here(b, carry, piece=piece, start=start):
            emitters(piece, start, b)
            return carry

        unroll = UNROLL if tiles_here % UNROLL == 0 else 1
        lax.fori_loop(0, tiles_here, emitters_here, 0, unroll=unroll)
        start += tiles_here

    def kinds_of(slot):
        return 3 if FROM_PRODUCT[slot % len(FROM_PRODUCT)] else 2

    def products_of(b, tiles, slot):
        rows_taken = kinds_of(slot) * CHUNK
        left = jnp.concatenate(
            [em[b, 3 * r : 3 * r + rows_taken] for r in range(0, TILE, CHUNK)], axis=0
        )
        right = jnp.concatenate([feat[:, lanes(a)] for a in tiles], axis=1)
        return jnp.dot(left, right, preferred_element_type=F32)

    def views(products, b, tiles, slot):
        kinds = kinds_of(slot)
        from_product = kinds == 3
        receive = [rows[:, lanes(a)] for a in tiles]
        for r in range(0, TILE, CHUNK):
            if not from_product:
                x, y, z = (
                    jnp.broadcast_to(place[b, r : r + CHUNK, k : k + 1], (CHUNK, TILE))
                    for k in range(3, 6)
                )
            for t in range(2):
                m = products[kinds * r : kinds * (r + CHUNK), t * TILE : (t + 1) * TILE]
                if from_product:
                    cos = m[2 * CHUNK :]
                else:
                    n = receive[t]
                    cos = n[3:4] * x + n[4:5] * y + n[5:6] * z + n[6:7]
                w = m[:CHUNK]
                v = jnp.maximum(cos, 0.0) * m[CHUNK : 2 * CHUNK]
                v = v * pltpu.reciprocal(w * w - 1.0, approx=True)
                at = slice(t * TILE, (t + 1) * TILE)
                view[slot, r : r + CHUNK, at] = jnp.maximum(v.astype(BF), 0)

    def add(b, tiles, slot):
        total = jnp.dot(rad[:, lanes(b)], view[slot], preferred_element_type=F32)
        for t, a in enumerate(tiles):
            out[:, lanes(jnp.minimum(a, n_rec - 1))] += total[:, t * TILE : (t + 1) * TILE]

    def step(i, carry):
        for j in range(STEP):
            add(*decoded(codes[jnp.maximum(i - 1, 0) * STEP + j]), j)
            tiles = decoded(codes[i * STEP + j])
            views(products_of(*tiles, j), *tiles, j)
        return carry

    lax.fori_loop(0, steps, step, 0)
    for j in range(STEP):
        add(*decoded(codes[jnp.maximum(steps - 1, 0) * STEP + j]), j)


def block_term(count, codes, own, *pieces):
    cases = pieces[0].shape[0] - own.shape[0]
    columns = sum(piece.shape[1] for piece in pieces)
    tiles = own.shape[1] // TILE
    smem = pl.BlockSpec(memory_space=pltpu.SMEM)
    vmem = pl.BlockSpec(memory_space=pltpu.VMEM)
    pairs = tiles * TILE * columns
    return pl.pallas_call(
        term_kernel,
        out_shape=jax.ShapeDtypeStruct((cases, tiles * TILE), F32),
        in_specs=[smem] * 2 + [vmem] * (1 + len(pieces)),
        out_specs=vmem,
        scratch_shapes=[
            pltpu.VMEM((FEATURES, (tiles + 1) * TILE), BF),
            pltpu.VMEM((8, (tiles + 1) * TILE), F32),
            pltpu.VMEM((cases, columns), BF),
            pltpu.VMEM((columns // TILE, 3 * TILE, FEATURES), BF),
            pltpu.VMEM((columns // TILE, TILE, FEATURES), F32),
            pltpu.VMEM((STEP, TILE, 2 * TILE), BF),
        ],
        compiler_params=pltpu.CompilerParams(vmem_limit_bytes=24 * 2**20),
        cost_estimate=pl.CostEstimate(
            flops=pairs * 300, bytes_accessed=8 * 2**20, transcendentals=pairs
        ),
        name="block_term",
    )(count, codes, own, *pieces)


def exchanged(block, axis, bits):
    return lax.ppermute(block, axis, [(i, i ^ bits) for i in range(lax.axis_size(axis))])


def spread_from(root, axis, wide, narrow):
    n = lax.axis_size(axis)
    me = lax.axis_index(axis)
    away, odd = me ^ root, me & 1
    wide = jnp.where(away & 1 == 0, wide, exchanged(wide, axis, 1))
    narrow = jnp.where(away & 1 == 0, narrow, exchanged(narrow, axis, 1))
    block = jnp.concatenate([wide, narrow], 0)
    q = block.shape[1] // 4
    parts = [
        jnp.where(odd == 0, block[:, i * q : (i + 1) * q], block[:, (i + 2) * q : (i + 3) * q])
        for i in range(2)
    ]
    bits = [1 << i for i in range(1, n.bit_length() - 1)]
    for pair in zip(bits, bits[::-1]):
        got = [exchanged(part, axis, bit) for part, bit in zip(parts, pair)]
        parts = [jnp.where(away & bit == 0, x, y) for x, y, bit in zip(parts, got, pair)]
    mine = jnp.concatenate(parts, axis=1)
    return mine, exchanged(mine, axis, 1)


def shifted(block, axis, distance):
    n = lax.axis_size(axis)
    return lax.ppermute(block, axis, [((i - distance) % n, i) for i in range(n)])


def on_device(positions, normals, areas, radiosity, reflect, partial_sums, visible, section):
    n_row = lax.axis_size("row")
    emit = (lax.axis_index("col") + section[0]) % n_row
    tiles = positions.shape[1] // TILE
    own = jnp.concatenate([positions, normals, areas[None], areas[None]], 0)
    pieces = spread_from(emit, "row", radiosity, own)
    carried = shifted(partial_sums, "col", 1)
    mask = lax.dynamic_slice_in_dim(visible, emit * tiles, tiles, 1)
    half = tiles // 2
    swapped = jnp.concatenate([mask[:, half:], mask[:, :half]], 1)
    mask = jnp.where(lax.axis_index("row") & 1 == 0, mask, swapped)
    count, codes = visible_pairs(mask)
    return carried + reflect[None, :] * block_term(count, codes, own, *pieces)


def solution(mesh):
    placed = (
        P(None, "row"),
        P(None, "row"),
        P("row"),
        P(None, "row"),
        P("row"),
        P("col", "row"),
        P("row", None),
        P(),
    )
    return jax.shard_map(
        on_device, mesh=mesh, in_specs=placed, out_specs=P("col", "row"), check_vma=False
    )
```

time: 82.5 us -> 77.8 us (0.943)
  Pallas kernels: 60.1 us -> 55.9 us
    pallas_call x1, Pallas kernels: 60.1 us -> 55.9 us  [block_term(): pl.pallas_call(term_kernel, out_shape=jax.ShapeDtypeStruct((cases, tiles...]
  transfers between devices with their start and end apart: 8 -> 8, of which waited for: 4 -> 4; matrix products, arithmetic and copies ran while one was open for 2% -> 3% of each run, Pallas kernels for 74% -> 72%
where the time goes in v1:
time: 77.8 us; the launch traced here: 77.5 us
  Pallas kernels  55.9 us (72%)
  starting transfers between devices  9.89 us (13%)
  waiting for transfers between devices  6.09 us (8%)
  other arithmetic  3.13 us (4%)
  local copies, waits for them, and re-layouts  1.41 us (2%)
  between operations  0.86 us (1%)
    pallas_call x1, Pallas kernels, block_term(): pl.pallas_call(term_kernel, out_shape=jax.ShapeDtypeStruct((cases, tiles...  55.9 us
    ppermute x7, starting transfers between devices, exchanged(): lax.ppermute(block, axis, [(i, i ^ bits) for i in range(lax.axis_size(axi...  6.88 us
    ppermute x7, waiting for transfers between devices, exchanged(): lax.ppermute(block, axis, [(i, i ^ bits) for i in range(lax.axis_size(axi...  6.09 us
    ppermute x1, starting transfers between devices, shifted(): lax.ppermute(block, axis, [((i - distance) % n, i) for i in range(n)])  3 us
  transfers between devices with their start and end apart: 8, of which 4 were waited for; matrix products, arithmetic and copies ran while one was open for 3% of the time, Pallas kernels for 72%

profile of v1, /device:TPU:0, one launch (start us, length us, event | category | flops | bytes accessed | tf_op | source)
XLA Modules:
  0.0 77.5 jit_solution(16991568360419430719)
XLA Ops:
  0.0 0.7 broadcast_in_dim.16
  0.7 0.0 copy-start.1
  0.7 1.0 %pad_maximum_fusion.2.own = bf16[8,6144]{1,0:T(8,128)(2,1)S(1)} fusion(bf16[1,6144]{1,0:T(2,128)(2,1)S(1)} %broadcast_in_dim.16, bf16[3,6144]{1,0:T(4,128)(2,1)} %param.9, bf16[3,6144]{1,0:T(4,128)(2,1)} %param.8), kind=kLoop, calls=%fused_computation.27 | loop fusion | flops 393216 | bytes 184320 | tf_op jit(solution)/shard_map/concatenate | solution.py:256
  1.7 0.5 collective-permute-start.2
  2.2 0.1 collective-permute-start.1
  2.3 3.0 %collective-permute-start = (f32[32,6144]{1,0:T(8,128)}, f32[32,6144]{1,0:T(8,128)S(1)}, u32[]{:S(2)}, u32[]{:S(2)}) collective-permute-start(f32[32,6144]{1,0:T(8,128)} %param.13), channel_id=1, source_target_pairs={{3,0},{0,1},{1,2},{2,3},{7,4},{4,5},{5,6},{6,7},{11,8},{8,9},{9,10... | collective-permute-start | bytes 2359304 | tf_op jit(solution)/shard_map/ppermute | solution.py:249
  6.0 0.0 copy-start
  6.0 0.1 constant_dynamic-slice_fusion
  6.1 0.1 fusion.8
  6.2 0.1 copy.11
  6.3 0.2 reduce_window_sum.18
  6.5 0.2 fusion.11
  6.7 0.1 reduce-window.4
  6.8 0.1 reduce
  6.9 0.1 convert_reduce_fusion.2
  7.0 0.1 select_reduce_fusion
  7.1 0.0 collective-permute-done.2
  7.3 0.1 fusion.4
  7.3 1.6 %collective-permute-start.3 = (bf16[40,1536]{1,0:T(8,128)(2,1)S(1)}, bf16[40,1536]{1,0:T(8,128)(2,1)S(1)}, u32[]{:S(2)}, u32[]{:S(2)}) collective-permute-start(bf16[40,1536]{1,0:T(8,128)(2,1)S(1)} %get-tuple-element.7), channel_id=1, source_target_pairs={{0,8},{4,12},{8,0},{12,4},{16,24},{20,28},{24,16},{28,20},{1,9},{5... | collective-permute-start | bytes 368648 | tf_op jit(solution)/shard_map/ppermute | solution.py:224
  8.9 1.5 %collective-permute-start.5 = (bf16[40,1536]{1,0:T(8,128)(2,1)S(1)}, bf16[40,1536]{1,0:T(8,128)(2,1)S(1)}, u32[]{:S(2)}, u32[]{:S(2)}) collective-permute-start(bf16[40,1536]{1,0:T(8,128)(2,1)S(1)} %get-tuple-element.8), channel_id=1, source_target_pairs={{0,16},{4,20},{8,24},{12,28},{16,0},{20,4},{24,8},{28,12},{1,17},{... | collective-permute-start | bytes 368648 | tf_op jit(solution)/shard_map/ppermute | solution.py:224
  10.4 2.0 %collective-permute-done.3 = bf16[40,1536]{1,0:T(8,128)(2,1)S(1)} collective-permute-done((bf16[40,1536]{1,0:T(8,128)(2,1)S(1)}, bf16[40,1536]{1,0:T(8,128)(2,1)S(1)}, u32[]{:S(2)}, u32[]{:S(2)}) %collective-permute-start.3) | collective-permute-done | bytes 122912 | tf_op jit(solution)/shard_map/ppermute | solution.py:224
  12.4 1.6 %collective-permute-start.4 = (bf16[40,1536]{1,0:T(8,128)(2,1)S(1)}, bf16[40,1536]{1,0:T(8,128)(2,1)S(1)}, u32[]{:S(2)}, u32[]{:S(2)}) collective-permute-start(bf16[40,1536]{1,0:T(8,128)(2,1)S(1)} %broadcast_select_fusion.2), channel_id=1, source_target_pairs={{0,16},{4,20},{8,24},{12,28},{16,0},{20,4},{24,8},{28,12},{1,17},{... | collective-permute-start | bytes 368648 | tf_op jit(solution)/shard_map/ppermute | solution.py:224
  14.0 1.6 %collective-permute-start.6 = (bf16[40,1536]{1,0:T(8,128)(2,1)S(1)}, bf16[40,1536]{1,0:T(8,128)(2,1)S(1)}, u32[]{:S(2)}, u32[]{:S(2)}) collective-permute-start(bf16[40,1536]{1,0:T(8,128)(2,1)S(1)} %broadcast_select_fusion.3), channel_id=1, source_target_pairs={{0,8},{4,12},{8,0},{12,4},{16,24},{20,28},{24,16},{28,20},{1,9},{5... | collective-permute-start | bytes 368648 | tf_op jit(solution)/shard_map/ppermute | solution.py:224
  15.6 1.8 %collective-permute-done.4 = bf16[40,1536]{1,0:T(8,128)(2,1)S(1)} collective-permute-done((bf16[40,1536]{1,0:T(8,128)(2,1)S(1)}, bf16[40,1536]{1,0:T(8,128)(2,1)S(1)}, u32[]{:S(2)}, u32[]{:S(2)}) %collective-permute-start.4) | collective-permute-done | bytes 122912 | tf_op jit(solution)/shard_map/ppermute | solution.py:224
  17.4 1.6 %collective-permute-done.6 = bf16[40,1536]{1,0:T(8,128)(2,1)S(1)} collective-permute-done((bf16[40,1536]{1,0:T(8,128)(2,1)S(1)}, bf16[40,1536]{1,0:T(8,128)(2,1)S(1)}, u32[]{:S(2)}, u32[]{:S(2)}) %collective-permute-start.6) | collective-permute-done | bytes 122912 | tf_op jit(solution)/shard_map/ppermute | solution.py:224
  19.0 0.1 collective-permute-start.7
  19.1 0.3 convert_reduce_fusion.1
  19.4 0.5 slice.37
  19.9 0.7 collective-permute-done.7.refs_1_
  20.6 55.9 %block_term.1 = f32[32,6144]{1,0:T(8,128)S(1)} custom-call(s32[1]{0:T(128)} %bitcast.2.count, s32[1200]{0:T(1024)S(1)} %shift-left_add_fusion.codes, bf16[8,6144]{1,0:T(8,128)(2,1)S(1)} %pad_maximum_fusion.2.own, bf16[40,3072]{1,0:T(8,128)(2,1)S(1)} %pad_maximum_fusion.refs_0_, bf16[40,3072]{1,0:T(8,128)(2,1)S(1)} %collective-permute-done.7.refs_1_), custom_call_target="tpu_custom_call" | custom-call | flops 11324620800 | bytes 8388608 | tf_op jit(solution)/shard_map/block_term/pallas_call | solution.py:202
  76.5 0.0 collective-permute-done
  76.5 1.0 %multiply_add_fusion = f32[32,6144]{1,0:T(8,128)} fusion(f32[32,6144]{1,0:T(8,128)S(1)} %collective-permute-done, f32[32,6144]{1,0:T(8,128)S(1)} %block_term.1, f32[6144]{0:T(1024)S(1)} %copy-done.2), kind=kLoop, calls=%fused_computation | loop fusion | flops 393216 | bytes 2383872 | tf_op jit(solution)/shard_map/add | solution.py:264
  (17 shorter events, 0.2 us)
Async XLA Ops:
  0.7 5.3 %copy-start.1 = (s32[48,384]{1,0:T(8,128)S(1)}, s32[48,384]{1,0:T(8,128)}, u32[]{:S(2)}) copy-start(s32[48,384]{1,0:T(8,128)} %param.14) | copy-start | bytes 221188
  1.7 5.4 %collective-permute-start.2 = (bf16[8,6144]{1,0:T(8,128)(2,1)S(1)}, bf16[8,6144]{1,0:T(8,128)(2,1)S(1)}, u32[]{:S(2)}, u32[]{:S(2)}) collective-permute-start(bf16[8,6144]{1,0:T(8,128)(2,1)S(1)} %pad_maximum_fusion.2.own), channel_id=1, source_target_pairs={{0,4},{4,0},{8,12},{12,8},{16,20},{20,16},{24,28},{28,24},{1,5},{5... | collective-permute-start | bytes 294920 | tf_op jit(solution)/shard_map/ppermute | solution.py:224
  2.2 5.0 %collective-permute-start.1 = (bf16[32,6144]{1,0:T(8,128)(2,1)}, bf16[32,6144]{1,0:T(8,128)(2,1)S(1)}, u32[]{:S(2)}, u32[]{:S(2)}) collective-permute-start(bf16[32,6144]{1,0:T(8,128)(2,1)} %param.11), channel_id=1, source_target_pairs={{0,4},{4,0},{8,12},{12,8},{16,20},{20,16},{24,28},{28,24},{1,5},{5... | collective-permute-start | bytes 1179656 | tf_op jit(solution)/shard_map/ppermute | solution.py:224
  2.3 74.2 %collective-permute-start = (f32[32,6144]{1,0:T(8,128)}, f32[32,6144]{1,0:T(8,128)S(1)}, u32[]{:S(2)}, u32[]{:S(2)}) collective-permute-start(f32[32,6144]{1,0:T(8,128)} %param.13), channel_id=1, source_target_pairs={{3,0},{0,1},{1,2},{2,3},{7,4},{4,5},{5,6},{6,7},{11,8},{8,9},{9,10... | collective-permute-start | bytes 2359304 | tf_op jit(solution)/shard_map/ppermute | solution.py:249
  6.0 1.2 %copy-start = (bf16[32,6144]{1,0:T(8,128)(2,1)S(1)}, bf16[32,6144]{1,0:T(8,128)(2,1)}, u32[]{:S(2)}) copy-start(bf16[32,6144]{1,0:T(8,128)(2,1)} %param.11) | copy-start | bytes 1179652
  7.3 5.1 %collective-permute-start.3 = (bf16[40,1536]{1,0:T(8,128)(2,1)S(1)}, bf16[40,1536]{1,0:T(8,128)(2,1)S(1)}, u32[]{:S(2)}, u32[]{:S(2)}) collective-permute-start(bf16[40,1536]{1,0:T(8,128)(2,1)S(1)} %get-tuple-element.7), channel_id=1, source_target_pairs={{0,8},{4,12},{8,0},{12,4},{16,24},{20,28},{24,16},{28,20},{1,9},{5... | collective-permute-start | bytes 368648 | tf_op jit(solution)/shard_map/ppermute | solution.py:224
  8.9 5.1 %collective-permute-start.5 = (bf16[40,1536]{1,0:T(8,128)(2,1)S(1)}, bf16[40,1536]{1,0:T(8,128)(2,1)S(1)}, u32[]{:S(2)}, u32[]{:S(2)}) collective-permute-start(bf16[40,1536]{1,0:T(8,128)(2,1)S(1)} %get-tuple-element.8), channel_id=1, source_target_pairs={{0,16},{4,20},{8,24},{12,28},{16,0},{20,4},{24,8},{28,12},{1,17},{... | collective-permute-start | bytes 368648 | tf_op jit(solution)/shard_map/ppermute | solution.py:224
  12.4 4.9 %collective-permute-start.4 = (bf16[40,1536]{1,0:T(8,128)(2,1)S(1)}, bf16[40,1536]{1,0:T(8,128)(2,1)S(1)}, u32[]{:S(2)}, u32[]{:S(2)}) collective-permute-start(bf16[40,1536]{1,0:T(8,128)(2,1)S(1)} %broadcast_select_fusion.2), channel_id=1, source_target_pairs={{0,16},{4,20},{8,24},{12,28},{16,0},{20,4},{24,8},{28,12},{1,17},{... | collective-permute-start | bytes 368648 | tf_op jit(solution)/shard_map/ppermute | solution.py:224
  14.0 4.9 %collective-permute-start.6 = (bf16[40,1536]{1,0:T(8,128)(2,1)S(1)}, bf16[40,1536]{1,0:T(8,128)(2,1)S(1)}, u32[]{:S(2)}, u32[]{:S(2)}) collective-permute-start(bf16[40,1536]{1,0:T(8,128)(2,1)S(1)} %broadcast_select_fusion.3), channel_id=1, source_target_pairs={{0,8},{4,12},{8,0},{12,4},{16,24},{20,28},{24,16},{28,20},{1,9},{5... | collective-permute-start | bytes 368648 | tf_op jit(solution)/shard_map/ppermute | solution.py:224
  19.0 1.6 %collective-permute-start.7 = (bf16[40,3072]{1,0:T(8,128)(2,1)S(1)}, bf16[40,3072]{1,0:T(8,128)(2,1)S(1)}, u32[]{:S(2)}, u32[]{:S(2)}) collective-permute-start(bf16[40,3072]{1,0:T(8,128)(2,1)S(1)} %pad_maximum_fusion.refs_0_), channel_id=1, source_target_pairs={{0,4},{4,0},{8,12},{12,8},{16,20},{20,16},{24,28},{28,24},{1,5},{5... | collective-permute-start | bytes 737288 | tf_op jit(solution)/shard_map/ppermute | solution.py:224
  20.6 55.9 %copy-start.2 = (f32[6144]{0:T(1024)S(1)}, f32[6144]{0:T(1024)}, u32[]{:S(2)}) copy-start(f32[6144]{0:T(1024)} %param.12) | copy-start | bytes 73732

commit v2 on v1

--- a/solution.py
+++ b/solution.py
@@ -36,7 +36,7 @@
     code = jnp.minimum(b, n_em - 1)
     for t in range(2):
         code = (code << BITS) + jnp.sum((rows <= rank[:, None] + t).astype(jnp.int32), axis=1)
-    return ends[-1:], code
+    return ends, code
 
 
 def decoded(code):
@@ -52,11 +52,11 @@
     return x.astype(BF).astype(F32)
 
 
-def term_kernel(count, codes, own, *refs):
+def term_kernel(ends, codes, own, *refs):
     pieces, (out, feat, rows, rad, em, place, view) = refs[:-7], refs[-7:]
     cases = out.shape[0]
     n_rec, n_em = own.shape[1] // TILE, rad.shape[1] // TILE
-    steps = (count[0] + STEP - 1) // STEP
+    steps = (ends[n_em - 1] + STEP - 1) // STEP
     out[...] = jnp.zeros_like(out)
     view[...] = jnp.zeros_like(view)
     feat[:, n_rec * TILE :] = jnp.zeros((FEATURES, TILE), BF)
@@ -117,14 +117,14 @@
         spot = jnp.concatenate([none[:3], px, py, pz, none[:2]], 0)
         ones = jnp.where((row >= 3) & (row < 6), 1.0, 0.0)
         facing = [spot, none, none, ones, none, none]
-        for kind, f in enumerate((wide, lit, facing)):
-            f = jnp.concatenate(f, 0).astype(BF)
-            columns = lax.dot_general(
-                turn, f, (((1,), (1,)), ((), ())), preferred_element_type=F32
-            )
-            if kind == 2:
-                place[start + b] = columns
-            columns = columns.astype(BF)
+        f = jnp.concatenate([*wide, none, none, *lit, none, none, *facing], 0).astype(BF)
+        columns = lax.dot_general(
+            turn, f, (((1,), (1,)), ((), ())), preferred_element_type=F32
+        )
+        kinds = [columns[:, :TILE], pltpu.roll(columns[:, :TILE], TILE // 2, 1), columns[:, TILE:]]
+        place[start + b] = kinds[2][:, :FEATURES]
+        for kind, columns in enumerate(kinds):
+            columns = columns[:, :FEATURES].astype(BF)
             for k in range(TILE // CHUNK):
                 at = (3 * k + kind) * CHUNK
                 em[start + b, at : at + CHUNK] = columns[k * CHUNK : (k + 1) * CHUNK]
@@ -192,7 +192,7 @@
         add(*decoded(codes[jnp.maximum(steps - 1, 0) * STEP + j]), j)
 
 
-def block_term(count, codes, own, *pieces):
+def block_term(ends, codes, own, *pieces):
     cases = pieces[0].shape[0] - own.shape[0]
     columns = sum(piece.shape[1] for piece in pieces)
     tiles = own.shape[1] // TILE
@@ -217,14 +217,14 @@
             flops=pairs * 300, bytes_accessed=8 * 2**20, transcendentals=pairs
         ),
         name="block_term",
-    )(count, codes, own, *pieces)
+    )(ends, codes, own, *pieces)
 
 
 def exchanged(block, axis, bits):
     return lax.ppermute(block, axis, [(i, i ^ bits) for i in range(lax.axis_size(axis))])
 
 
-def spread_from(root, axis, wide, narrow):
+def spread_from(root, axis, wide, narrow, later):
     n = lax.axis_size(axis)
     me = lax.axis_index(axis)
     away, odd = me ^ root, me & 1
@@ -240,8 +240,10 @@
     for pair in zip(bits, bits[::-1]):
         got = [exchanged(part, axis, bit) for part, bit in zip(parts, pair)]
         parts = [jnp.where(away & bit == 0, x, y) for x, y, bit in zip(parts, got, pair)]
+        if pair[0] == bits[0]:
+            parts, later = lax.optimization_barrier((parts, later))
     mine = jnp.concatenate(parts, axis=1)
-    return mine, exchanged(mine, axis, 1)
+    return (mine, exchanged(mine, axis, 1)), later
 
 
 def shifted(block, axis, distance):
@@ -254,14 +256,15 @@
     emit = (lax.axis_index("col") + section[0]) % n_row
     tiles = positions.shape[1] // TILE
     own = jnp.concatenate([positions, normals, areas[None], areas[None]], 0)
-    pieces = spread_from(emit, "row", radiosity, own)
-    carried = shifted(partial_sums, "col", 1)
     mask = lax.dynamic_slice_in_dim(visible, emit * tiles, tiles, 1)
     half = tiles // 2
     swapped = jnp.concatenate([mask[:, half:], mask[:, :half]], 1)
     mask = jnp.where(lax.axis_index("row") & 1 == 0, mask, swapped)
-    count, codes = visible_pairs(mask)
-    return carried + reflect[None, :] * block_term(count, codes, own, *pieces)
+    ends, codes = visible_pairs(mask)
+    later = (partial_sums, ends, codes)
+    pieces, (partial_sums, ends, codes) = spread_from(emit, "row", radiosity, own, later)
+    carried = shifted(partial_sums, "col", 1)
+    return carried + reflect[None, :] * block_term(ends, codes, own, *pieces)
 
 
 def solution(mesh):

time: 77.8 us -> 76.6 us (0.985)
  the two profiles are of different devices: /device:TPU:0 before, /device:TPU:27 now
where the time goes in v2:
time: 76.6 us; the launch traced here: 75.8 us
  Pallas kernels  56.2 us (73%)
  waiting for transfers between devices  8.46 us (11%)
  starting transfers between devices  6.01 us (8%)
  other arithmetic  3.08 us (4%)
  local copies, waits for them, and re-layouts  0.91 us (1%)
  between operations  0.86 us (1%)
    pallas_call x1, Pallas kernels, block_term(): pl.pallas_call(term_kernel, out_shape=jax.ShapeDtypeStruct((cases, tiles...  56.2 us
    ppermute x7, waiting for transfers between devices, exchanged(): lax.ppermute(block, axis, [(i, i ^ bits) for i in range(lax.axis_size(axi...  8.46 us
    ppermute x7, starting transfers between devices, exchanged(): lax.ppermute(block, axis, [(i, i ^ bits) for i in range(lax.axis_size(axi...  6.01 us
  transfers between devices with their start and end apart: 8, of which 5 were waited for; matrix products, arithmetic and copies ran while one was open for 2% of the time, Pallas kernels for 74%

profile of v2, /device:TPU:27, one launch (start us, length us, event | category | flops | bytes accessed | tf_op | source)
XLA Modules:
  0.0 75.8 jit_solution(13001125947762654075)
XLA Ops:
  0.0 0.7 broadcast_in_dim.10
  0.7 0.0 copy-start.1
  0.7 1.0 %pad_maximum_fusion.2.own = bf16[8,6144]{1,0:T(8,128)(2,1)S(1)} fusion(bf16[1,6144]{1,0:T(2,128)(2,1)S(1)} %broadcast_in_dim.10, bf16[3,6144]{1,0:T(4,128)(2,1)} %param.9, bf16[3,6144]{1,0:T(4,128)(2,1)} %param.8), kind=kLoop, calls=%fused_computation.27 | loop fusion | flops 393216 | bytes 184320 | tf_op jit(solution)/shard_map/concatenate | solution.py:258
  1.7 0.7 collective-permute-start.1
  2.5 0.1 collective-permute-start
  3.2 0.1 constant_dynamic-slice_fusion
  3.3 0.1 fusion.8
  3.4 0.1 copy.11
  3.5 0.2 reduce_window_sum.18
  3.7 0.2 fusion.11
  3.9 0.1 reduce-window.7
  4.0 0.1 reduce.ends
  4.1 0.1 convert_reduce_fusion.2
  4.2 0.1 select_reduce_fusion
  4.4 0.3 convert_reduce_fusion.1
  4.7 0.0 collective-permute-done
  4.7 0.0 copy-done
  4.7 0.1 fusion.2
  4.8 1.3 %collective-permute-start.3 = (bf16[40,1536]{1,0:T(8,128)(2,1)S(1)}, bf16[40,1536]{1,0:T(8,128)(2,1)S(1)}, u32[]{:S(2)}, u32[]{:S(2)}) collective-permute-start(bf16[40,1536]{1,0:T(8,128)(2,1)S(1)} %get-tuple-element.17), channel_id=1, source_target_pairs={{0,16},{4,20},{8,24},{12,28},{16,0},{20,4},{24,8},{28,12},{1,17},{... | collective-permute-start | bytes 368648 | tf_op jit(solution)/shard_map/ppermute | solution.py:224
  6.1 0.3 collective-permute-start.2
  6.4 3.0 %collective-permute-done.3 = bf16[40,1536]{1,0:T(8,128)(2,1)S(1)} collective-permute-done((bf16[40,1536]{1,0:T(8,128)(2,1)S(1)}, bf16[40,1536]{1,0:T(8,128)(2,1)S(1)}, u32[]{:S(2)}, u32[]{:S(2)}) %collective-permute-start.3) | collective-permute-done | bytes 122912 | tf_op jit(solution)/shard_map/ppermute | solution.py:224
  9.4 0.0 copy-start.3
  9.4 0.9 %collective-permute-done.2 = bf16[40,1536]{1,0:T(8,128)(2,1)S(1)} collective-permute-done((bf16[40,1536]{1,0:T(8,128)(2,1)S(1)}, bf16[40,1536]{1,0:T(8,128)(2,1)S(1)}, u32[]{:S(2)}, u32[]{:S(2)}) %collective-permute-start.2) | collective-permute-done | bytes 122912 | tf_op jit(solution)/shard_map/ppermute | solution.py:224
  10.3 0.4 collective-permute-start.5
  10.7 0.3 collective-permute-start.6
  11.0 3.1 %collective-permute-done.5 = bf16[40,1536]{1,0:T(8,128)(2,1)S(1)} collective-permute-done((bf16[40,1536]{1,0:T(8,128)(2,1)S(1)}, bf16[40,1536]{1,0:T(8,128)(2,1)S(1)}, u32[]{:S(2)}, u32[]{:S(2)}) %collective-permute-start.5) | collective-permute-done | bytes 122912 | tf_op jit(solution)/shard_map/ppermute | solution.py:224
  14.1 0.3 collective-permute-done.6
  14.5 0.0 copy-start.2
  14.5 3.0 %collective-permute-start.7 = (bf16[40,3072]{1,0:T(8,128)(2,1)S(1)}, bf16[40,3072]{1,0:T(8,128)(2,1)S(1)}, u32[]{:S(2)}, u32[]{:S(2)}) collective-permute-start(bf16[40,3072]{1,0:T(8,128)(2,1)S(1)} %pad_maximum_fusion.refs_0_), channel_id=1, source_target_pairs={{0,4},{4,0},{8,12},{12,8},{16,20},{20,16},{24,28},{28,24},{1,5},{5... | collective-permute-start | bytes 737288 | tf_op jit(solution)/shard_map/ppermute | solution.py:224
  17.5 1.1 %collective-permute-done.7.refs_1_ = bf16[40,3072]{1,0:T(8,128)(2,1)S(1)} collective-permute-done((bf16[40,3072]{1,0:T(8,128)(2,1)S(1)}, bf16[40,3072]{1,0:T(8,128)(2,1)S(1)}, u32[]{:S(2)}, u32[]{:S(2)}) %collective-permute-start.7) | collective-permute-done | bytes 245792 | tf_op jit(solution)/shard_map/ppermute | solution.py:224
  18.6 56.2 %block_term.1 = f32[32,6144]{1,0:T(8,128)S(1)} custom-call(s32[48]{0:T(128)S(1)} %reduce.ends, s32[1200]{0:T(1024)S(1)} %shift-left_add_fusion.codes, bf16[8,6144]{1,0:T(8,128)(2,1)S(1)} %pad_maximum_fusion.2.own, bf16[40,3072]{1,0:T(8,128)(2,1)S(1)} %pad_maximum_fusion.refs_0_, bf16[40,3072]{1,0:T(8,128)(2,1)S(1)} %collective-permute-done.7.refs_1_), custom_call_target="tpu_custom_call" | custom-call | flops 11324620800 | bytes 8388608 | tf_op jit(solution)/shard_map/block_term/pallas_call | solution.py:202
  74.8 1.0 %multiply_add_fusion = f32[32,6144]{1,0:T(8,128)} fusion(f32[32,6144]{1,0:T(8,128)S(1)} %collective-permute-done.4, f32[32,6144]{1,0:T(8,128)S(1)} %block_term.1, f32[6144]{0:T(1024)S(1)} %copy-done.2), kind=kLoop, calls=%fused_computation | loop fusion | flops 393216 | bytes 2383872 | tf_op jit(solution)/shard_map/add | solution.py:267
  (18 shorter events, 0.2 us)
Async XLA Ops:
  0.7 2.5 %copy-start.1 = (s32[48,384]{1,0:T(8,128)S(1)}, s32[48,384]{1,0:T(8,128)}, u32[]{:S(2)}) copy-start(s32[48,384]{1,0:T(8,128)} %param.14) | copy-start | bytes 221188
  1.7 2.9 %collective-permute-start.1 = (bf16[8,6144]{1,0:T(8,128)(2,1)S(1)}, bf16[8,6144]{1,0:T(8,128)(2,1)S(1)}, u32[]{:S(2)}, u32[]{:S(2)}) collective-permute-start(bf16[8,6144]{1,0:T(8,128)(2,1)S(1)} %pad_maximum_fusion.2.own), channel_id=1, source_target_pairs={{0,4},{4,0},{8,12},{12,8},{16,20},{20,16},{24,28},{28,24},{1,5},{5... | collective-permute-start | bytes 294920 | tf_op jit(solution)/shard_map/ppermute | solution.py:224
  2.5 2.2 %collective-permute-start = (bf16[32,6144]{1,0:T(8,128)(2,1)}, bf16[32,6144]{1,0:T(8,128)(2,1)S(1)}, u32[]{:S(2)}, u32[]{:S(2)}) collective-permute-start(bf16[32,6144]{1,0:T(8,128)(2,1)} %param.11), channel_id=1, source_target_pairs={{0,4},{4,0},{8,12},{12,8},{16,20},{20,16},{24,28},{28,24},{1,5},{5... | collective-permute-start | bytes 1179656 | tf_op jit(solution)/shard_map/ppermute | solution.py:224
  3.7 1.0 %copy-start = (bf16[32,6144]{1,0:T(8,128)(2,1)S(1)}, bf16[32,6144]{1,0:T(8,128)(2,1)}, u32[]{:S(2)}) copy-start(bf16[32,6144]{1,0:T(8,128)(2,1)} %param.11) | copy-start | bytes 1179652
  4.8 4.5 %collective-permute-start.3 = (bf16[40,1536]{1,0:T(8,128)(2,1)S(1)}, bf16[40,1536]{1,0:T(8,128)(2,1)S(1)}, u32[]{:S(2)}, u32[]{:S(2)}) collective-permute-start(bf16[40,1536]{1,0:T(8,128)(2,1)S(1)} %get-tuple-element.17), channel_id=1, source_target_pairs={{0,16},{4,20},{8,24},{12,28},{16,0},{20,4},{24,8},{28,12},{1,17},{... | collective-permute-start | bytes 368648 | tf_op jit(solution)/shard_map/ppermute | solution.py:224
  6.1 4.1 %collective-permute-start.2 = (bf16[40,1536]{1,0:T(8,128)(2,1)S(1)}, bf16[40,1536]{1,0:T(8,128)(2,1)S(1)}, u32[]{:S(2)}, u32[]{:S(2)}) collective-permute-start(bf16[40,1536]{1,0:T(8,128)(2,1)S(1)} %get-tuple-element.18), channel_id=1, source_target_pairs={{0,8},{4,12},{8,0},{12,4},{16,24},{20,28},{24,16},{28,20},{1,9},{5... | collective-permute-start | bytes 368648 | tf_op jit(solution)/shard_map/ppermute | solution.py:224
  9.4 8.1 %copy-start.3 = (f32[32,6144]{1,0:T(8,128)S(1)}, f32[32,6144]{1,0:T(8,128)}, u32[]{:S(2)}) copy-start(f32[32,6144]{1,0:T(8,128)} %param.13) | copy-start | bytes 2359300
  10.3 3.8 %collective-permute-start.5 = (bf16[40,1536]{1,0:T(8,128)(2,1)S(1)}, bf16[40,1536]{1,0:T(8,128)(2,1)S(1)}, u32[]{:S(2)}, u32[]{:S(2)}) collective-permute-start(bf16[40,1536]{1,0:T(8,128)(2,1)S(1)} %broadcast_select_fusion.4), channel_id=1, source_target_pairs={{0,16},{4,20},{8,24},{12,28},{16,0},{20,4},{24,8},{28,12},{1,17},{... | collective-permute-start | bytes 368648 | tf_op jit(solution)/shard_map/ppermute | solution.py:224
  10.7 3.7 %collective-permute-start.6 = (bf16[40,1536]{1,0:T(8,128)(2,1)S(1)}, bf16[40,1536]{1,0:T(8,128)(2,1)S(1)}, u32[]{:S(2)}, u32[]{:S(2)}) collective-permute-start(bf16[40,1536]{1,0:T(8,128)(2,1)S(1)} %broadcast_select_fusion.2), channel_id=1, source_target_pairs={{0,8},{4,12},{8,0},{12,4},{16,24},{20,28},{24,16},{28,20},{1,9},{5... | collective-permute-start | bytes 368648 | tf_op jit(solution)/shard_map/ppermute | solution.py:224
  14.5 60.4 %copy-start.2 = (f32[6144]{0:T(1024)S(1)}, f32[6144]{0:T(1024)}, u32[]{:S(2)}) copy-start(f32[6144]{0:T(1024)} %param.12) | copy-start | bytes 73732
  14.5 4.1 %collective-permute-start.7 = (bf16[40,3072]{1,0:T(8,128)(2,1)S(1)}, bf16[40,3072]{1,0:T(8,128)(2,1)S(1)}, u32[]{:S(2)}, u32[]{:S(2)}) collective-permute-start(bf16[40,3072]{1,0:T(8,128)(2,1)S(1)} %pad_maximum_fusion.refs_0_), channel_id=1, source_target_pairs={{0,4},{4,0},{8,12},{12,8},{16,20},{20,16},{24,28},{28,24},{1,5},{5... | collective-permute-start | bytes 737288 | tf_op jit(solution)/shard_map/ppermute | solution.py:224
  17.5 57.4 %collective-permute-start.4 = (f32[32,6144]{1,0:T(8,128)S(1)}, f32[32,6144]{1,0:T(8,128)S(1)}, u32[]{:S(2)}, u32[]{:S(2)}) collective-permute-start(f32[32,6144]{1,0:T(8,128)S(1)} %copy-done.3), channel_id=1, source_target_pairs={{3,0},{0,1},{1,2},{2,3},{7,4},{4,5},{5,6},{6,7},{11,8},{8,9},{9,10... | collective-permute-start | bytes 2359304 | tf_op jit(solution)/shard_map/ppermute | solution.py:251
